TPU v7x, 128 devices: a whole 4x4x4 slice. The times are simulated.
128 devices in a mesh: grp: 8 (over y, core), sub: 16 (over z, x).
Axes of the slice: x: 4, y: 4, z: 4, core: 2. Of those that a mesh axis runs over, the one named last changes fastest.
Arguments:
- feats: bfloat16 [1024, 8, 8, 512], P(('grp', 'sub')), may hold values from -6 to 6
- neighbours: int32 [1024, 6], P(('grp', 'sub')), may hold values from -1 to 1023, as said below
- w_fine: bfloat16 [7, 64, 64], replicated, may hold values from -0.25 to 0.25
- w_down: bfloat16 [512, 256], replicated, may hold values from -0.25 to 0.25
- w_lift: bfloat16 [256, 512], replicated, may hold values from -0.375 to 0.375
- coarse_nbrs: int32 [128, 6], replicated, may hold values from -1 to 127, as said below
- w_coarse: bfloat16 [7, 512, 512], replicated, may hold values from -0.09375 to 0.09375
- w_back: bfloat16 [512, 256], replicated, may hold values from -0.25 to 0.25
- w_up: bfloat16 [256, 512], replicated, may hold values from -0.375 to 0.375
- grad_out: bfloat16 [1024, 8, 8, 512], P(('grp', 'sub')), may hold values from -6 to 6
Outputs:
- fine_out: bfloat16 [1024, 8, 8, 512], P(('grp', 'sub'))
- feats_grad: bfloat16 [1024, 8, 8, 512], P(('grp', 'sub'))
- w_fine_grad: float32 [7, 64, 64], replicated
- w_down_grad: float32 [512, 256], replicated
- w_lift_grad: float32 [256, 512], replicated
- w_coarse_grad: float32 [7, 512, 512], replicated
- w_back_grad: float32 [512, 256], replicated
- w_up_grad: float32 [256, 512], replicated
Inputs may be any that keep to these rules, and one draw needn't show every extreme that they name: `neighbours`: each entry is -1 or a brick of the same device or of a device at most 2 away in the device order of the bricks (device i holds bricks i*8 to (i+1)*8 - 1); one device's entries name bricks of one other device at most 6 times, and exactly 6 times for some other device. `coarse_nbrs`: each entry is -1 or a node.
All inputs are finite; a program needn't handle non-finite values.
Results may differ from a plain program's by a relative error of at most 0.012.
Values may be sent and summed in bfloat16 or wider, within the bound.
A program may use at most 128 MiB of HBM per device.

v0:
```python
import functools

import jax
import jax.numpy as jnp
from jax import lax
from jax.experimental import pallas as pl
from jax.experimental.pallas import tpu as pltpu
from jax.sharding import PartitionSpec as P

F32 = jnp.float32
BF16 = jnp.bfloat16
I32 = jnp.int32
MESH = pl.DeviceIdType.MESH
OFFSETS = (-2, -1, 1, 2)
MEMORY = 58 << 20
ENTRIES = 48
SOURCES = ENTRIES + 32
SLOTS = 6


def dot(x, y):
    return jnp.dot(x, y, preferred_element_type=F32)


def dot_nt(x, y):
    return lax.dot_general(x, y, (((1,), (1,)), ((), ())), preferred_element_type=F32)


def dot_tn(x, y):
    return lax.dot_general(x, y, (((0,), (0,)), ((), ())), preferred_element_type=F32)


def sigmoid(v):
    return 1.0 / (1.0 + jnp.exp(-v))


def perm_index(y):
    a, e = (y >> 8) & 1, (y >> 7) & 1
    u, w, b = (y >> 5) & 3, (y >> 3) & 3, y & 7
    return b * 64 + (2 * u + a) * 8 + 2 * w + e


def perm_to():
    rows = lax.broadcasted_iota(jnp.int32, (512, 512), 0)
    cols = lax.broadcasted_iota(jnp.int32, (512, 512), 1)
    return (perm_index(rows) == cols).astype(F32).astype(BF16)


def perm_from():
    rows = lax.broadcasted_iota(jnp.int32, (512, 512), 0)
    cols = lax.broadcasted_iota(jnp.int32, (512, 512), 1)
    return (perm_index(cols) == rows).astype(F32).astype(BF16)


def load_natural(ref):
    return ref[...].astype(F32).reshape(512, 512).astype(BF16)


def pooled_rows(x, perm, out_ref, wide_ref=None):
    y = dot(perm, x)
    for z in range(4):
        for ae in range(4):
            block = y[ae * 128 : (ae + 1) * 128, z * 128 : (z + 1) * 128]
            where = (pl.ds(z * 128, 128), pl.ds(ae * 128, 128))
            out_ref[where] = block.astype(BF16)
            if wide_ref is not None:
                wide_ref[where] = block


def natural_rows(q, perm_back):
    y = jnp.concatenate(
        [
            jnp.concatenate(
                [q[z * 128 : (z + 1) * 128, ae * 128 : (ae + 1) * 128] for z in range(4)], axis=1
            )
            for ae in range(4)
        ],
        axis=0,
    )
    return dot(perm_back, y).reshape(64, 8, 512).astype(BF16)


def low_lanes(rows):
    return lax.broadcasted_iota(jnp.int32, (rows, 128), 1) < 64


def layer(ref, axis, place, parity):
    if axis == 0:
        return jnp.concatenate(
            [
                ref[z * 128 + place * 32 : z * 128 + place * 32 + 32, parity * 256 : parity * 256 + 256]
                for z in range(4)
            ],
            axis=0,
        )
    if axis == 1:
        parts = []
        for a in range(2):
            lane = (a * 2 + parity) * 128
            parts.append(
                jnp.concatenate(
                    [ref[zu * 32 + place * 8 : zu * 32 + place * 8 + 8, lane : lane + 128] for zu in range(16)],
                    axis=0,
                )
            )
        return jnp.concatenate(parts, axis=1)
    parts = []
    for a in range(2):
        first = ref[place * 128 : place * 128 + 128, a * 256 : a * 256 + 128]
        second = ref[place * 128 : place * 128 + 128, a * 256 + 128 : a * 256 + 256]
        if parity == 0:
            second = pltpu.roll(second, 64, 1)
        else:
            first = pltpu.roll(first, 64, 1)
        parts.append(jnp.where(low_lanes(128), first, second))
    return jnp.concatenate(parts, axis=1)


def add_layer(ref, axis, place, parity, value):
    if axis == 0:
        for z in range(4):
            rows = pl.ds(z * 128 + place * 32, 32)
            ref[rows, parity * 256 : parity * 256 + 256] += value[z * 32 : z * 32 + 32]
    elif axis == 1:
        for a in range(2):
            lane = (a * 2 + parity) * 128
            for zu in range(16):
                rows = pl.ds(zu * 32 + place * 8, 8)
                ref[rows, lane : lane + 128] += value[zu * 8 : zu * 8 + 8, a * 128 : a * 128 + 128]
    else:
        low = low_lanes(128)
        rows = pl.ds(place * 128, 128)
        for a in range(2):
            part = value[:, a * 128 : a * 128 + 128]
            turned = pltpu.roll(part, 64, 1)
            first, second = (part, turned) if parity == 0 else (turned, part)
            keep = low if parity == 0 else ~low
            ref[rows, a * 256 : a * 256 + 128] += jnp.where(keep, first, 0.0)
            ref[rows, a * 256 + 128 : a * 256 + 256] += jnp.where(keep, second, 0.0)


FACES = ((0, 3, 1), (0, 0, 0), (1, 3, 1), (1, 0, 0), (2, 3, 1), (2, 0, 0))
BEYOND = ((0, 3, 0), (0, 0, 1), (1, 3, 0), (1, 0, 1), (2, 3, 0), (2, 0, 1))


def one_hot(mask):
    return mask.astype(F32).astype(BF16)


def iota(rows, cols, axis):
    return lax.broadcasted_iota(jnp.int32, (rows, cols), axis)


def entries(neighbours, me):
    nb = neighbours[...]
    n = jnp.concatenate([jnp.broadcast_to(nb[:, d : d + 1], (8, 128)) for d in range(6)], axis=0)
    lane = iota(ENTRIES, 128, 1)
    direction = iota(ENTRIES, 128, 0) >> 3
    offset = (n >> 3) - me
    number = (direction ^ 1) * 8 + (n & 7)
    local = (n >= 0) & (offset == 0)
    peer = lane >> 3
    peer_offset = jnp.where(peer < 2, peer - 2, peer - 1)
    far = (n >= 0) & (lane < 32) & (offset == peer_offset)
    before = one_hot(iota(ENTRIES, ENTRIES, 1) < iota(ENTRIES, ENTRIES, 0))
    count = dot(before, one_hot(far))
    slot = far & (count == (lane & 7).astype(F32))
    place = jnp.sum(jnp.where(slot, lane + 1, 0), axis=1, keepdims=True)
    source = jnp.where(local, number, jnp.where(place > 0, ENTRIES - 1 + place, SOURCES))
    return one_hot(local & (lane == number)), one_hot(slot), number, source


def rolled(x, by):
    return pltpu.roll(x.astype(F32), by, 1).astype(BF16)


def coords(groups, subs, offset):
    nodes = groups * subs
    at = lax.axis_index("grp") * subs + lax.axis_index("sub")
    to = lax.rem(at + offset + nodes, nodes)
    return (to // subs, lax.rem(to, subs))


def ring(a, b, size):
    return min((a - b) % size, (b - a) % size)


def peers_of(groups, subs):
    g, s = lax.axis_index("grp"), lax.axis_index("sub")
    near = [coords(groups, subs, off) for off in OFFSETS]
    y, core = g // 2, lax.rem(g, 2)
    steps = [(dy, dc) for dy in range(groups // 2) for dc in range(2) if dy or dc]
    steps.sort(key=lambda d: -4 * ring(d[0], 0, groups // 2) - d[1])
    over_grp = [(lax.rem(y + dy, groups // 2) * 2 + lax.rem(core + dc, 2), s) for dy, dc in steps]
    wide = min(4, subs)
    deep = subs // wide
    z, x = s // wide, lax.rem(s, wide)
    steps = [(dz, dx) for dz in range(deep) for dx in range(wide) if dz or dx]
    steps.sort(key=lambda d: -ring(d[0], 0, deep) - ring(d[1], 0, wide))
    over_sub = [(g, lax.rem(z + dz, deep) * wide + lax.rem(x + dx, wide)) for dz, dx in steps]
    return near, over_grp, over_sub


def squares(groups, subs):
    g, s = lax.axis_index("grp"), lax.axis_index("sub")
    ys, deep = groups // 2, subs // 4
    y, core = g // 2, lax.rem(g, 2)
    z, x = s // 4, lax.rem(s, 4)
    low, high = (x ^ (x >> 1)) & 1, x >> 1
    steps = [(d, f) for d in range(ys) for f in range(2) if d or f]
    steps.sort(key=lambda d: -ring(d[0], 0, ys) - d[1])
    first = [(lax.rem(y + d, ys) * 2 + core, z * 4 + (x ^ f)) for d, f in steps]
    first_rank = [lax.rem(y + d, ys) * 2 + (low ^ f) for d, f in steps]
    heard_rank = [lax.rem(y + ys - d, ys) * 2 + (low ^ f) for d, f in steps]
    steps = [(d, f) for d in range(deep) for f in range(2) if d or f]
    steps.sort(key=lambda d: -ring(d[0], 0, deep) - d[1])
    second = [(g, lax.rem(z + d, deep) * 4 + (x ^ (3 * f))) for d, f in steps]
    return first, first_rank, heard_rank, y * 2 + low, second, z * 2 + high


def greet(peers):
    barrier = pltpu.get_barrier_semaphore()
    for peer in peers:
        pl.semaphore_signal(barrier, inc=1, device_id=peer, device_id_type=MESH)
    return lambda: pl.semaphore_wait(barrier, len(peers))


def send_all(peers, sems, src_of, dst_of):
    copies = []
    for k, peer in enumerate(peers):
        copy = pltpu.make_async_remote_copy(
            src_ref=src_of(k, peer),
            dst_ref=dst_of(k, peer),
            send_sem=sems.at[0, k],
            recv_sem=sems.at[1, k],
            device_id=peer,
            device_id_type=MESH,
        )
        copy.start()
        copies.append(copy)
    return copies


def send_near(near, sems, src, dst):
    copies = []
    for p in (0, 3, 1, 2):
        copy = pltpu.make_async_remote_copy(
            src_ref=src.at[p],
            dst_ref=dst.at[3 - p],
            send_sem=sems.at[0, p],
            recv_sem=sems.at[1, 3 - p],
            device_id=near[p],
            device_id_type=MESH,
        )
        copy.start()
        copies.append(copy)
    return copies


def copy_all(pairs, sems, first):
    copies = []
    for k, (src, dst) in enumerate(pairs):
        copy = pltpu.make_async_copy(src, dst, sems.at[first + k])
        copy.start()
        copies.append(copy)
    return copies


def wait_all(copies):
    for copy in copies:
        copy.wait()


def by_place(layers):
    return jnp.concatenate([x.reshape(16, 8, 256) for x in layers], axis=1).astype(BF16)


def by_brick(layers, stage, out):
    for which, value in enumerate(layers):
        for half in range(2):
            lanes = slice(half * 128, half * 128 + 128)
            stage[which, half] = value[:, lanes]
            for b in range(8):
                out[which * 8 + b, :, lanes] = stage[which, half, pl.ds(b, 16, stride=8), :].astype(BF16)


def pick_slots(numbers, faces, out):
    for p in range(4):
        for i in range(SLOTS):
            row = jnp.clip(numbers[p * 8 + i, 0] - 1, 0, ENTRIES - 1)
            out[p, i] = faces[row]


def unpack_slots(slots, spread, table):
    for p in range(4):
        for i in range(SLOTS):
            face = slots[p, i].astype(F32)
            for half in range(2):
                spread[half, pl.ds(p * 8 + i, 16, stride=32), :] = face[:, half * 128 : half * 128 + 128]
    for half in range(2):
        table[:, ENTRIES:SOURCES, half * 128 : half * 128 + 128] = (
            spread[half].reshape(16, 32, 128).astype(BF16)
        )


def build_mats(w_fine, m0, mx, my, mz):
    zero = jnp.zeros((128, 128), BF16)
    none = jnp.zeros((64, 64), BF16)

    def put(ref, i, j, value):
        ref[i * 128 : (i + 1) * 128, j * 128 : (j + 1) * 128] = value

    def quad(a, b, c, d):
        return jnp.concatenate(
            [jnp.concatenate([a, b], axis=1), jnp.concatenate([c, d], axis=1)], axis=0
        )

    w = [w_fine[t] for t in range(7)]
    c = quad(w[0], w[6], w[5], w[0])
    d1, d2, d3, d4 = (quad(w[t], none, none, w[t]) for t in range(1, 5))
    ez = quad(none, w[5], w[6], none)
    for a in range(2):
        for e in range(2):
            i = a * 2 + e
            put(m0, i, i, c)
            put(m0, i, (1 - a) * 2 + e, d1 if a == 1 else d2)
            put(m0, i, a * 2 + (1 - e), d3 if e == 1 else d4)
            put(m0, i, 3 - i, zero)
    for i in range(2):
        for j in range(2):
            put(mx.at[0], i, j, d1 if i == j else zero)
            put(mx.at[1], i, j, d2 if i == j else zero)
            put(mz, i, j, ez if i == j else zero)
    put(my, 0, 0, zero)
    put(my, 1, 1, zero)
    put(my, 0, 1, d3)
    put(my, 1, 0, d4)


def block_kernel(
    groups, subs,
    feats_in, grad_in, neighbours, w_fine, w_down_in, w_up_in, nbrs, w_lift_in, w_coarse_in, w_back_in,
    fine_to, feats_grad, up_all, down_all, fine_all, taps_to, mean_to, grad_to, coarse_to, dpre_to, in_to, back_to, sum_to,
    feats, grad, w_down, w_up, w_lift, w_coarse, w_back,
    fine_out, taps_out, out_mean, out_grad, out_coarse, out_dpre, out_in, out_back, out_sum,
    q, g, sx, sy, sz, hidden, slope, pooled, pool_slope, grad_merged, slab, back_add,
    wide, faces, border, table, slot_wide, spread_out, rim, asked, wanted, source_of, entry_of,
    asked_at, source_at, entry_at, send, send_2, recv_2, m0, mx, my, mz, base, node, first, pack,
    flat, taps, inner, merged, dpre, x_back, y_back, z_back,
    up_parts, up_core, up_mid, up_in, up_slots, down_parts, down_core, down_mid, down_in, down_slots,
    fine_parts, fine_core, fine_mid, fine_in, fine_slots,
    sems_in, sems_out, sems_s, sems_a, sems_b, sems_c, sems_d, sems_n,
    up_a, up_b, up_c, up_d, up_e, down_a, down_b, down_c, down_d, down_e, fine_a, fine_b, fine_c, fine_d, fine_e,
):
    gi, si = lax.axis_index("grp"), lax.axis_index("sub")
    near, over_grp, over_sub = peers_of(groups, subs)
    over_a, rank_a, heard, ai, over_b, bi = squares(groups, subs)
    na, nb = len(over_a) + 1, len(over_b) + 1
    ci = lax.rem(gi, 2)
    twin = [(gi + 1 - 2 * ci, si)]
    greeted = greet(near + over_grp + over_sub + over_a)
    up_rows, down_rows, fine_rows = 256 // na, 512 // na, 128 // na

    def add(own, incoming, copies):
        wait_all(copies)
        value = own.astype(F32)
        for k in range(len(copies)):
            value = value + incoming[k].astype(F32)
        return value.astype(BF16)

    def join(slots, copies, count):
        wait_all(copies)
        value = slots[0].astype(F32)
        for k in range(1, count):
            value = value + slots[k].astype(F32)
        return value.astype(BF16)

    def to_twin(parts, core_in, sems):
        return send_all(twin, sems, lambda k, peer: parts.at[1 - ci], lambda k, peer: core_in)

    def over_chips(parts, core_in, mid, incoming, copies, sems):
        wait_all(copies)
        mid[...] = (parts[ci].astype(F32) + core_in[...].astype(F32)).astype(BF16)
        return send_all(over_a, sems, lambda k, peer: mid.at[rank_a[k]], lambda k, peer: incoming.at[k])

    def across(mid, incoming, slots, copies, sems):
        slots[bi] = add(mid[ai], incoming, copies)
        return send_all(over_b, sems, lambda k, peer: slots.at[bi], lambda k, peer: slots.at[bi])

    def spread(slots, everything, copies, sems):
        everything[ci, ai] = join(slots, copies, nb)
        return send_all(
            over_a, sems, lambda k, peer: everything.at[ci, ai], lambda k, peer: everything.at[ci, ai]
        )

    def share(everything, copies, sems):
        sent = []
        for k in range(na):
            if k > 0:
                copies[k - 1].wait_recv()
            part = everything.at[ci, ai if k == 0 else heard[k - 1]]
            copy = pltpu.make_async_remote_copy(
                src_ref=part,
                dst_ref=part,
                send_sem=sems.at[0, k],
                recv_sem=sems.at[1, k],
                device_id=twin[0],
                device_id_type=MESH,
            )
            copy.start()
            sent.append(copy)
        for copy in copies:
            copy.wait_send()
        return sent

    loads = copy_all(
        ((feats_in, feats), (grad_in, grad), (w_up_in, w_up), (w_down_in, w_down)), sems_in, 0
    )
    local, slot, number, source = entries(neighbours, gi * subs + si)
    wanted[...] = dot_tn(slot, (number + 1).astype(F32).astype(BF16))[0:32].reshape(4, 8, 128).astype(jnp.int32)
    greeted()
    asking = send_near(near, sems_a, wanted, asked)
    entry = (iota(ENTRIES, 128, 0) + 1).astype(F32).astype(BF16)
    entry_of[...] = dot_tn(slot, entry)[0:32].astype(jnp.int32)
    source_of[...] = source
    numbers = copy_all(((source_of, source_at), (entry_of, entry_at)), sems_s, 0)
    loads += copy_all(
        ((w_lift_in, w_lift), (w_coarse_in, w_coarse), (w_back_in, w_back)), sems_in, len(loads)
    )

    perm = perm_to()
    loads[0].wait()
    pooled_rows(load_natural(feats), perm, q, wide)
    by_brick([layer(wide, *where) for where in FACES], rim, border)
    faces[SOURCES] = jnp.zeros((16, 256), BF16)
    wait_all(asking)
    asked_copy = copy_all(((asked, asked_at),), sems_s, 2)
    eye = one_hot(iota(ENTRIES, 128, 0) == iota(ENTRIES, 128, 1))
    given = one_hot(asked[...].reshape(32, 128) - 1 == iota(32, 128, 1))
    wait_all(asked_copy)
    for p in range(4):
        for i in range(SLOTS):
            row = jnp.clip(asked_at[p, i, 0] - 1, 0, ENTRIES - 1)
            send[p, i] = border[row]
    sending = []
    for p in (0, 3, 1, 2):
        copy = pltpu.make_async_remote_copy(
            src_ref=send.at[p],
            dst_ref=faces.at[pl.ds(ENTRIES + (3 - p) * 8, SLOTS)],
            send_sem=sems_b.at[0, p],
            recv_sem=sems_b.at[1, 3 - p],
            device_id=near[p],
            device_id_type=MESH,
        )
        copy.start()
        sending.append(copy)

    local_back = dot_tn(local, eye)[0:ENTRIES].astype(BF16)
    given_back = dot_tn(given, eye[0:32])[0:ENTRIES].astype(BF16)
    back_add[...] = local_back + rolled(given_back, ENTRIES)
    spread_out[...] = jnp.zeros_like(spread_out)
    faces[0:ENTRIES] = border[...]
    loads[1].wait()
    pooled_rows(load_natural(grad), perm, g)
    build_mats(w_fine, m0, mx, my, mz)
    base[...] = dot(q[...], m0[...])
    loads[2].wait()
    merged_grad = dot_nt(g[...], w_up[...])
    grad_merged[...] = merged_grad
    total = jnp.sum(g[...].astype(F32), axis=0, keepdims=True).astype(BF16).astype(F32)
    low = low_lanes(512)
    for z in range(4):
        at = z * 128
        sx[at : at + 96, 0:256] = q[at + 32 : at + 128, 0:256]
        sx[at + 32 : at + 128, 256:512] = q[at : at + 96, 256:512]
    wait_all(numbers)
    loads[3].wait()

    wait_all(sending)
    for d in range(6):
        for b in range(8):
            row = jnp.clip(source_at[d * 8 + b, 0], 0, SOURCES)
            face = faces[row].astype(F32)
            for half in range(2):
                rim[d, half, pl.ds(b, 16, stride=8), :] = face[:, half * 128 : half * 128 + 128]
    for z in range(4):
        at = z * 128
        for half in range(2):
            first_lanes, last_lanes = slice(half * 128, half * 128 + 128), slice(half * 128 + 256, half * 128 + 384)
            sx[at + 96 : at + 128, first_lanes] = rim[0, half, z * 32 : z * 32 + 32, :].astype(BF16)
            sx[at : at + 32, last_lanes] = rim[1, half, z * 32 : z * 32 + 32, :].astype(BF16)
    for a in range(2):
        lanes = slice(a * 256, a * 256 + 128)
        part = wide[:, lanes].reshape(16, 32, 128)
        edge = rim[2, a].reshape(16, 8, 128)
        sy[:, lanes] = jnp.concatenate([part[:, 8:], edge], axis=1).reshape(512, 128).astype(BF16)
        lanes = slice(a * 256 + 128, a * 256 + 256)
        part = wide[:, lanes].reshape(16, 32, 128)
        edge = rim[3, a].reshape(16, 8, 128)
        sy[:, lanes] = jnp.concatenate([edge, part[:, :24]], axis=1).reshape(512, 128).astype(BF16)
        above, below = rim[4, a], rim[5, a]
        for e in range(2):
            lanes = slice((a * 2 + e) * 128, (a * 2 + e) * 128 + 128)
            part = wide[:, lanes]
            edge_up = above if e == 0 else pltpu.roll(above, 64, 1)
            edge_down = pltpu.roll(below, 64, 1) if e == 0 else below
            up = jnp.concatenate([part[128:], edge_up], axis=0)
            down = jnp.concatenate([edge_down, part[:384]], axis=0)
            sz[:, lanes] = jnp.where(low, up, down).astype(BF16)
    for a in range(2):
        lanes = slice(a * 256, a * 256 + 256)
        other = slice(256 - a * 256, 512 - a * 256)
        pre = (
            base[:, lanes]
            + dot(sx[:, other], mx[1 - a])
            + dot(sy[:, lanes], my[...])
            + dot(sz[:, lanes], mz[...])
        )
        s = sigmoid(pre)
        hidden[:, lanes] = (pre * s).astype(BF16)
        slope[:, lanes] = s * (1.0 + pre * (1.0 - s))
    pre = dot(hidden[...], w_down[...])
    s = sigmoid(pre)
    value = (pre * s).astype(BF16)
    mean = jnp.sum(value.astype(F32), axis=0, keepdims=True) * (1.0 / 512.0)
    mean = mean.astype(BF16).astype(F32)
    for k in range(2):
        node[k : k + 1, :] = mean[:, k * 128 : k * 128 + 128]
    for k in range(4):
        node[2 + k : 3 + k, :] = total[:, k * 128 : k * 128 + 128]
    sending = send_all(over_grp, sems_c, lambda k, peer: node, lambda k, peer: first.at[gi])
    pooled[...] = value
    pool_slope[...] = s * (1.0 + pre * (1.0 - s))
    first[gi] = node[...]
    part = dot_tn(value, g[...])
    for c in range(2):
        for i in range(na):
            for k in range(2):
                up_parts[c, i, k * up_rows : (k + 1) * up_rows, :] = part[
                    i * up_rows : (i + 1) * up_rows, c * 256 + k * 128 : c * 256 + (k + 1) * 128
                ].astype(BF16)
    up_sent = to_twin(up_parts, up_core, up_a)
    wait_all(sending)
    for i in range(groups):
        pack[6 * i : 6 * i + 6, :] = first[i]
    slab[si] = pack[...].astype(BF16)
    sending = send_all(over_sub, sems_d, lambda k, peer: slab.at[si], lambda k, peer: slab.at[si])
    wait_all(sending)
    up_sent = over_chips(up_parts, up_core, up_mid, up_in, up_sent, up_b)

    nodes = groups * subs
    me = gi * subs + si
    for s in range(subs):
        flat[s * groups * 6 : (s + 1) * groups * 6, :] = slab[s].astype(F32)
    pieces = [flat[pl.ds(k, nodes, stride=6), :] for k in range(6)]
    rows, cols = iota(nodes, nodes, 0), iota(nodes, nodes, 1)
    order = one_hot(lax.rem(rows, subs) * groups + rows // subs == cols)
    gathered = dot(order, jnp.concatenate(pieces, axis=1).astype(BF16)).astype(BF16)
    node_mean, grad_sum = gathered[:, :256], gathered[:, 256:]
    node_grad = dot_nt(grad_sum, w_up[...]).astype(BF16)
    wait_all(loads[4:])
    coarse_in = dot(node_mean, w_lift[...]).astype(BF16)
    picks = [one_hot(nbrs[d : d + 1, :] == rows) for d in range(6)]
    taps[:, 0:512] = coarse_in
    for d in range(6):
        taps[:, (d + 1) * 512 : (d + 2) * 512] = dot_tn(picks[d], coarse_in).astype(BF16)
    coarse_pre = jnp.zeros((nodes, 512), F32)
    for t in range(7):
        coarse_pre = coarse_pre + dot(taps[:, t * 512 : (t + 1) * 512], w_coarse[t])
    s = sigmoid(coarse_pre)
    coarse_out = (coarse_pre * s).astype(BF16)
    coarse_slope = s * (1.0 + coarse_pre * (1.0 - s))
    coarse_dpre = (dot_nt(node_grad, w_back[...]) * coarse_slope).astype(BF16)
    in_grad = dot_nt(coarse_dpre, w_coarse[0])
    for d in range(6):
        moved = dot(picks[d], coarse_dpre).astype(BF16)
        in_grad = in_grad + dot_nt(moved, w_coarse[d + 1])
    in_grad = in_grad.astype(BF16)
    mine = one_hot(iota(16, nodes, 1) == me)
    mean_grad = dot_nt(dot(mine, in_grad).astype(BF16), w_lift[...])[0:1] * (1.0 / 512.0)


    pool_dpre = ((grad_merged[...] + mean_grad) * pool_slope[...]).astype(BF16)
    part = dot_tn(hidden[...], pool_dpre)
    for c in range(2):
        down_parts[c] = part[:, c * 128 : (c + 1) * 128].reshape(na, down_rows, 128).astype(BF16)
    down_sent = to_twin(down_parts, down_core, down_a)
    up_sent = across(up_mid, up_in, up_slots, up_sent, up_c)
    dpre[...] = ((g[...].astype(F32) + dot_nt(pool_dpre, w_down[...])) * slope[...]).astype(BF16)

    def block(value, i, j):
        return value[i * 128 : (i + 1) * 128, j * 128 : (j + 1) * 128]

    def fold(value):
        return value[:64] + pltpu.roll(value[64:], 64, 1)

    down_sent = over_chips(down_parts, down_core, down_mid, down_in, down_sent, down_b)
    centre = dot_tn(q[...], dpre[...])
    gx0 = dot_tn(sx[:, 0:256], dpre[:, 256:512])
    gx1 = dot_tn(sx[:, 256:512], dpre[:, 0:256])
    gy = [dot_tn(sy[:, a * 256 : a * 256 + 256], dpre[:, a * 256 : a * 256 + 256]) for a in range(2)]
    gz = [dot_tn(sz[:, a * 256 : a * 256 + 256], dpre[:, a * 256 : a * 256 + 256]) for a in range(2)]
    middle = sum(block(centre, i, i) for i in range(4))
    x_up = block(centre, 2, 0) + block(centre, 3, 1) + block(gx0, 0, 0) + block(gx0, 1, 1)
    x_down = block(centre, 0, 2) + block(centre, 1, 3) + block(gx1, 0, 0) + block(gx1, 1, 1)
    y_up = block(centre, 1, 0) + block(centre, 3, 2) + block(gy[0], 0, 1) + block(gy[1], 0, 1)
    y_down = block(centre, 0, 1) + block(centre, 2, 3) + block(gy[0], 1, 0) + block(gy[1], 1, 0)
    between = sum(block(value, i, i) for value in gz for i in range(2))
    z_up = middle[64:] + pltpu.roll(between[:64], 64, 1)
    z_down = pltpu.roll(middle[:64], 64, 1) + between[64:]
    tap_sums = [fold(middle), fold(x_up), fold(x_down), fold(y_up), fold(y_down), z_up, z_down]
    tap_sums.append(jnp.zeros((64, 128), F32))
    low = low_lanes(64)
    for pair in range(4):
        both = jnp.where(low, tap_sums[2 * pair], pltpu.roll(tap_sums[2 * pair + 1], 64, 1))
        each = fine_rows if fine_rows < 64 else 64
        for i in range(64 // each):
            row = pair * 64 + i * each
            half, at = row // 128, row % 128
            fine_parts[half, at // fine_rows, at % fine_rows : at % fine_rows + each, :] = both[
                i * each : (i + 1) * each
            ].astype(BF16)
    fine_sent = to_twin(fine_parts, fine_core, fine_a)

    x_back[:, 0:256] = dot_nt(dpre[:, 256:512], mx[0])
    x_back[:, 256:512] = dot_nt(dpre[:, 0:256], mx[1])
    for a in range(2):
        lanes = slice(a * 256, a * 256 + 256)
        y_back[:, lanes] = dot_nt(dpre[:, lanes], my[...])
        z_back[:, lanes] = dot_nt(dpre[:, lanes], mz[...])
    fine_sent = over_chips(fine_parts, fine_core, fine_mid, fine_in, fine_sent, fine_b)
    down_sent = across(down_mid, down_in, down_slots, down_sent, down_c)
    backs = (x_back, y_back, z_back)
    layers = [layer(backs[where[0]], *where) for where in BEYOND]
    by_brick(layers, rim, border)
    pick_slots(entry_at, border, send_2)
    slots_sent = send_near(near, sems_n, send_2, recv_2)
    fine_sent = across(fine_mid, fine_in, fine_slots, fine_sent, fine_c)
    up_sent = spread(up_slots, up_all, up_sent, up_d)
    down_sent = spread(down_slots, down_all, down_sent, down_d)
    table[:, 0:ENTRIES, :] = by_place(layers)
    for ref, value in (
        (out_mean, node_mean), (out_grad, node_grad), (out_coarse, coarse_out),
        (out_dpre, coarse_dpre), (out_in, in_grad),
        (out_back, dot(coarse_out, w_back[...]).astype(BF16)), (out_sum, grad_sum),
    ):
        ref[...] = value
    stores = copy_all(
        (
            (out_dpre, dpre_to), (out_mean, mean_to), (out_grad, grad_to),
            (out_coarse, coarse_to), (out_in, in_to), (out_back, back_to), (out_sum, sum_to),
        ),
        sems_out,
        0,
    )

    turned = dot_tn(coarse_in, one_hot(rows == cols)).astype(BF16)
    taps_out[0:512, :] = turned
    for d in range(6):
        taps_out[(d + 1) * 512 : (d + 2) * 512, :] = dot(turned, picks[d]).astype(BF16)
    stores += copy_all(((taps_out, taps_to),), sems_out, len(stores))
    back = dot(dot(mine, coarse_out).astype(BF16), w_back[...])[0:1]
    merged[...] = (pooled[...].astype(F32) + back).astype(BF16)
    inner[...] = g[...].astype(F32) + dot_nt(dpre[...], m0[...])
    fine_sent = spread(fine_slots, fine_all, fine_sent, fine_d)

    for z in range(4):
        at = z * 128
        inner[at + 32 : at + 128, 0:256] += x_back[at : at + 96, 0:256]
        inner[at : at + 96, 256:512] += x_back[at + 32 : at + 128, 256:512]
    for zu in range(16):
        at = zu * 32
        for a in range(2):
            low_half, high_half = slice(a * 256, a * 256 + 128), slice(a * 256 + 128, a * 256 + 256)
            inner[at + 8 : at + 32, low_half] += y_back[at : at + 24, low_half]
            inner[at : at + 24, high_half] += y_back[at + 8 : at + 32, high_half]
    low = low_lanes(384)
    for i in range(4):
        lanes = slice(i * 128, i * 128 + 128)
        inner[128:512, lanes] += jnp.where(low, z_back[0:384, lanes], 0.0)
        inner[0:384, lanes] += jnp.where(low, 0.0, z_back[128:512, lanes])
    back_perm = perm_from()
    out = q[...].astype(F32) + hidden[...].astype(F32) + dot(merged[...], w_up[...])
    fine_out[...] = natural_rows(out.astype(BF16), back_perm)
    stores += copy_all(((fine_out, fine_to),), sems_out, len(stores))

    up_sent = share(up_all, up_sent, up_e)
    down_sent = share(down_all, down_sent, down_e)
    wait_all(slots_sent)
    unpack_slots(recv_2, spread_out, table)
    for place in range(16):
        slot_wide[place] = dot(back_add[:, 0:SOURCES], table[place])
    for f in range(6):
        add_layer(inner, *FACES[f], slot_wide[:, f * 8 : f * 8 + 8, :].reshape(128, 256))
    feats_grad[...] = natural_rows(inner[...].astype(BF16), back_perm)
    fine_sent = share(fine_all, fine_sent, fine_e)
    wait_all(up_sent)
    wait_all(fine_sent)
    wait_all(down_sent)
    wait_all(stores)


def finish_kernel(
    groups, subs,
    fine_in, feats_in, up_in, down_in, fine_sum_in, taps_in, mean_in, grad_in, coarse_in, dpre_in, in_grad_in, back_in, sum_in,
    fine_to, feats_to, w_fine_to, w_down_to, w_lift_to, w_coarse_to, w_back_to, w_up_to,
    fine_out, feats_out, up_all, down_all, fine_all, taps, node_mean, node_grad, coarse_out, dpre, in_grad, back, grad_sum,
    w_fine_grad, w_down_grad, w_lift_grad, w_coarse_grad, w_back_grad, w_up_grad,
    sems_in, sems_out,
):
    first = copy_all(
        ((dpre_in, dpre),) + tuple((taps_in.at[pl.ds(t * 512, 512)], taps.at[pl.ds(t * 512, 512)]) for t in range(7)),
        sems_in,
        0,
    )
    rest = copy_all(
        (
            (back_in, back), (sum_in, grad_sum), (up_in, up_all), (down_in, down_all), (fine_sum_in, fine_all), (coarse_in, coarse_out),
            (grad_in, node_grad), (mean_in, node_mean), (in_grad_in, in_grad), (fine_in, fine_out), (feats_in, feats_out),
        ),
        sems_in,
        8,
    )
    stores = []

    def store(src, dst):
        stores.extend(copy_all(((src, dst),), sems_out, len(stores)))

    first[0].wait()
    for t in range(7):
        first[t + 1].wait()
        w_coarse_grad[t] = dot(taps[t * 512 : (t + 1) * 512, :], dpre[...])
        store(w_coarse_grad.at[t], w_coarse_to.at[t])
    na = groups
    up_rows = 256 // na
    wait_all(rest[0:3])
    w_up_grad[...] = dot_tn(back[...], grad_sum[...])
    for c in range(2):
        for i in range(na):
            for k in range(2):
                w_up_grad[i * up_rows : (i + 1) * up_rows, c * 256 + k * 128 : c * 256 + (k + 1) * 128] += up_all[
                    c, i, k * up_rows : (k + 1) * up_rows, :
                ].astype(F32)
    store(w_up_grad, w_up_to)
    rest[3].wait()
    for c in range(2):
        w_down_grad[:, c * 128 : (c + 1) * 128] = down_all[c].astype(F32).reshape(512, 128)
    store(w_down_grad, w_down_to)
    rest[4].wait()
    sums = fine_all[...].astype(F32).reshape(256, 128)
    for pair in range(4):
        both = sums[pair * 64 : (pair + 1) * 64]
        w_fine_grad[2 * pair] = both[:, 0:64]
        if pair < 3:
            w_fine_grad[2 * pair + 1] = pltpu.roll(both, 64, 1)[:, 0:64]
    store(w_fine_grad, w_fine_to)
    wait_all(rest[5:9])
    w_back_grad[...] = dot_tn(coarse_out[...], node_grad[...])
    store(w_back_grad, w_back_to)
    w_lift_grad[...] = dot_tn(node_mean[...], in_grad[...])
    store(w_lift_grad, w_lift_to)
    rest[9].wait()
    store(fine_out, fine_to)
    rest[10].wait()
    store(feats_out, feats_to)
    wait_all(stores)


def spec(space=pltpu.VMEM):
    return pl.BlockSpec(memory_space=space)


def shape(dims, dtype):
    return jax.ShapeDtypeStruct(dims, dtype)


def buf(dims, dtype=BF16):
    return pltpu.VMEM(dims, dtype)


def pairs(count):
    return pltpu.SemaphoreType.DMA((2, count))


def body(groups, subs, feats, neighbours, w_fine, w_down, w_lift, coarse_nbrs, w_coarse, w_back, w_up, grad_out):
    nodes = groups * subs
    vmem, anywhere = spec(), spec(pl.ANY)
    sq16, sq32 = buf((512, 512)), buf((512, 512), F32)
    natural = shape((64, 8, 512), BF16)
    na, nb = groups, subs // 2
    chunk, fine_chunk = (512 // na, 128), (128 // na, 128)
    sums = (
        shape((2, na) + chunk, BF16), shape((2, na) + chunk, BF16), shape((2, na) + fine_chunk, BF16),
    )
    coarse = (
        shape((7 * 512, nodes), BF16), shape((nodes, 256), BF16), shape((nodes, 256), BF16),
        shape((nodes, 512), BF16), shape((nodes, 512), BF16), shape((nodes, 512), BF16),
        shape((nodes, 256), BF16), shape((nodes, 512), BF16),
    )
    slots = buf((4, SLOTS, 16, 256))

    def reduction(part):
        return [
            buf((2, na) + part), buf((na,) + part), buf((na,) + part), buf((na - 1,) + part), buf((nb,) + part),
        ]

    reduction_sems = [pairs(1), pairs(na - 1), pairs(nb - 1), pairs(na - 1), pairs(na)]

    def like(x):
        return buf(x.shape, x.dtype)

    results = pl.pallas_call(
        functools.partial(block_kernel, groups, subs),
        out_shape=(natural, natural) + sums + coarse,
        in_specs=[anywhere, anywhere, vmem, vmem, anywhere, anywhere, vmem, anywhere, anywhere, anywhere],
        out_specs=(anywhere,) + (vmem,) * 4 + (anywhere,) * 8,
        scratch_shapes=[like(natural), like(natural)]
        + [buf((512, 256)), buf((256, 512)), buf((256, 512)), buf((7, 512, 512)), buf((512, 256))]
        + [like(natural)]
        + [like(x) for x in coarse]
        + [sq16] * 6
        + [sq32, buf((512, 256)), buf((512, 256), F32), buf((512, 256), F32)]
        + [buf((subs, groups * 6, 128)), buf((ENTRIES, 128))]
        + [sq32, buf((SOURCES + 1, 16, 256)), buf((ENTRIES, 16, 256))]
        + [buf((16, SOURCES, 256)), buf((16, ENTRIES, 256), F32), buf((2, 512, 128), F32), buf((6, 2, 128, 128), F32)]
        + [buf((4, 8, 128), I32), buf((4, 8, 128), I32), buf((ENTRIES, 128), I32), buf((32, 128), I32)]
        + [pltpu.SMEM((4, 8, 128), I32), pltpu.SMEM((ENTRIES, 128), I32), pltpu.SMEM((32, 128), I32)]
        + [slots, slots, slots]
        + [sq16, buf((2, 256, 256)), buf((256, 256)), buf((256, 256))]
        + [sq32, buf((6, 128), F32), buf((groups, 6, 128), F32), buf((groups * 6, 128), F32)]
        + [buf((nodes * 6, 128), F32), buf((nodes, 7 * 512)), sq32, buf((512, 256)), sq16, sq32, sq32, sq32]
        + reduction(chunk)
        + reduction(chunk)
        + reduction(fine_chunk)
        + [pltpu.SemaphoreType.DMA((7,)), pltpu.SemaphoreType.DMA((9,)), pltpu.SemaphoreType.DMA((3,))]
        + [pairs(4), pairs(4), pairs(groups - 1), pairs(subs - 1), pairs(4)]
        + reduction_sems * 3,
        compiler_params=pltpu.CompilerParams(collective_id=1, has_side_effects=True, vmem_limit_bytes=MEMORY),
        name="block",
    )(
        feats.reshape(64, 8, 512), grad_out.reshape(64, 8, 512), neighbours,
        w_fine, w_down, w_up, coarse_nbrs.T, w_lift, w_coarse, w_back,
    )

    grads = (
        shape((7, 64, 64), F32), shape((512, 256), F32), shape((256, 512), F32),
        shape((7, 512, 512), F32), shape((512, 256), F32), shape((256, 512), F32),
    )
    outs = pl.pallas_call(
        functools.partial(finish_kernel, groups, subs),
        out_shape=(natural, natural) + grads,
        in_specs=[anywhere] * 13,
        out_specs=(anywhere,) * 8,
        scratch_shapes=[like(natural), like(natural)]
        + [like(x) for x in sums + coarse + grads]
        + [pltpu.SemaphoreType.DMA((19,)), pltpu.SemaphoreType.DMA((14,))],
        compiler_params=pltpu.CompilerParams(vmem_limit_bytes=MEMORY),
        name="finish",
    )(*results)
    return (outs[0].reshape(8, 8, 8, 512), outs[1].reshape(8, 8, 8, 512)) + tuple(outs[2:])


def solution(mesh):
    groups, subs = mesh.shape["grp"], mesh.shape["sub"]
    split4 = P(("grp", "sub"), None, None, None)
    return jax.shard_map(
        functools.partial(body, groups, subs),
        mesh=mesh,
        in_specs=(split4, P(("grp", "sub"), None)) + (P(),) * 7 + (split4,),
        out_specs=(split4, split4) + (P(),) * 6,
        check_vma=False,
    )
```

profile of v0, /device:TPU:1, one launch (start us, length us, event | category | flops | bytes accessed | tf_op | source)
XLA Modules:
  0.0 64.2 jit_solution(13587865344648000382)
XLA Ops:
  0.6 58.1 %block.1 = (bf16[64,8,512]{2,1,0:T(8,128)(2,1)}, bf16[64,8,512]{2,1,0:T(8,128)(2,1)}, bf16[2,8,64,128]{3,2,1,0:T(8,128)(2,1)}, bf16[2,8,64,128]{3,2,1,0:T(8,128)...) custom-call(bf16[64,8,512]{2,1,0:T(8,128)(2,1)} %bitcast.5, ...), custom_call_target="tpu_custom_call" | custom-call | tf_op jit(solution)/shard_map/block/pallas_call | solution.py:812
  58.7 5.5 %finish.1 = (bf16[64,8,512]{2,1,0:T(8,128)(2,1)}, bf16[64,8,512]{2,1,0:T(8,128)(2,1)}, f32[7,64,64]{2,1,0:T(8,128)}, f32[512,256]{1,0:T(8,128)}, f32[256,512]{1,...) custom-call(bf16[64,8,512]{2,1,0:T(8,128)(2,1)} %get-tuple-element.29.fine_in, ...), custom_call_target="tpu_custom_call" | custom-call | tf_op jit(solution)/shard_map/finish/pallas_call | solution.py:849
where the time goes:
time: 64.4 us; the launch traced here: 64.2 us
  Pallas kernels  63.6 us (99%)
    pallas_call x1, Pallas kernels, body(): pl.pallas_call(functools.partial(block_kernel, groups, subs), out_shape=(...  58.1 us
    pallas_call x1, Pallas kernels, body(): pl.pallas_call(functools.partial(finish_kernel, groups, subs), out_shape=...  5.52 us

commit v1 on v0

--- a/solution.py
+++ b/solution.py
@@ -340,9 +340,9 @@
 def block_kernel(
     groups, subs,
     feats_in, grad_in, neighbours, w_fine, w_down_in, w_up_in, nbrs, w_lift_in, w_coarse_in, w_back_in,
-    fine_to, feats_grad, up_all, down_all, fine_all, taps_to, mean_to, grad_to, coarse_to, dpre_to, in_to, back_to, sum_to,
+    fine_to, feats_to, up_to, down_to, fine_sum_to, taps_to, mean_to, grad_to, coarse_to, dpre_to, in_to, back_to, sum_to,
     feats, grad, w_down, w_up, w_lift, w_coarse, w_back,
-    fine_out, taps_out, out_mean, out_grad, out_coarse, out_dpre, out_in, out_back, out_sum,
+    fine_out, feats_grad, up_all, down_all, fine_all, taps_out, out_mean, out_grad, out_coarse, out_dpre, out_in, out_back, out_sum,
     q, g, sx, sy, sz, hidden, slope, pooled, pool_slope, grad_merged, slab, back_add,
     wide, faces, border, table, slot_wide, spread_out, rim, asked, wanted, source_of, entry_of,
     asked_at, source_at, entry_at, send, send_2, recv_2, m0, mx, my, mz, base, node, first, pack,
@@ -693,10 +693,13 @@
     for f in range(6):
         add_layer(inner, *FACES[f], slot_wide[:, f * 8 : f * 8 + 8, :].reshape(128, 256))
     feats_grad[...] = natural_rows(inner[...].astype(BF16), back_perm)
+    stores += copy_all(((feats_grad, feats_to),), sems_out, len(stores))
     fine_sent = share(fine_all, fine_sent, fine_e)
-    wait_all(up_sent)
-    wait_all(fine_sent)
-    wait_all(down_sent)
+    for copies, src, dst in (
+        (up_sent, up_all, up_to), (down_sent, down_all, down_to), (fine_sent, fine_all, fine_sum_to),
+    ):
+        wait_all(copies)
+        stores += copy_all(((src, dst),), sems_out, len(stores))
     wait_all(stores)
 
 
@@ -813,11 +816,11 @@
         functools.partial(block_kernel, groups, subs),
         out_shape=(natural, natural) + sums + coarse,
         in_specs=[anywhere, anywhere, vmem, vmem, anywhere, anywhere, vmem, anywhere, anywhere, anywhere],
-        out_specs=(anywhere,) + (vmem,) * 4 + (anywhere,) * 8,
+        out_specs=(anywhere,) * 13,
         scratch_shapes=[like(natural), like(natural)]
         + [buf((512, 256)), buf((256, 512)), buf((256, 512)), buf((7, 512, 512)), buf((512, 256))]
-        + [like(natural)]
-        + [like(x) for x in coarse]
+        + [like(natural), like(natural)]
+        + [like(x) for x in sums + coarse]
         + [sq16] * 6
         + [sq32, buf((512, 256)), buf((512, 256), F32), buf((512, 256), F32)]
         + [buf((subs, groups * 6, 128)), buf((ENTRIES, 128))]
@@ -832,7 +835,7 @@
         + reduction(chunk)
         + reduction(chunk)
         + reduction(fine_chunk)
-        + [pltpu.SemaphoreType.DMA((7,)), pltpu.SemaphoreType.DMA((9,)), pltpu.SemaphoreType.DMA((3,))]
+        + [pltpu.SemaphoreType.DMA((7,)), pltpu.SemaphoreType.DMA((13,)), pltpu.SemaphoreType.DMA((3,))]
         + [pairs(4), pairs(4), pairs(groups - 1), pairs(subs - 1), pairs(4)]
         + reduction_sems * 3,
         compiler_params=pltpu.CompilerParams(collective_id=1, has_side_effects=True, vmem_limit_bytes=MEMORY),

time: 64.4 us -> 64 us (level)
  no operation moved by 1% of the time
where the time goes in v1:
time: 64 us; the launch traced here: 63.9 us
  Pallas kernels  63.2 us (99%)
  between operations  0.64 us (1%)
    pallas_call x1, Pallas kernels, body(): pl.pallas_call(functools.partial(block_kernel, groups, subs), out_shape=(...  57.7 us
    pallas_call x1, Pallas kernels, body(): pl.pallas_call(functools.partial(finish_kernel, groups, subs), out_shape=...  5.52 us

profile of v1, /device:TPU:1, one launch (start us, length us, event | category | flops | bytes accessed | tf_op | source)
XLA Modules:
  0.0 63.9 jit_solution(301077450160997282)
XLA Ops:
  0.6 57.7 %block.1 = (bf16[64,8,512]{2,1,0:T(8,128)(2,1)}, bf16[64,8,512]{2,1,0:T(8,128)(2,1)}, bf16[2,8,64,128]{3,2,1,0:T(8,128)(2,1)}, bf16[2,8,64,128]{3,2,1,0:T(8,128)...) custom-call(bf16[64,8,512]{2,1,0:T(8,128)(2,1)} %bitcast.5, ...), custom_call_target="tpu_custom_call" | custom-call | tf_op jit(solution)/shard_map/block/pallas_call | solution.py:815
  58.3 5.5 %finish.1 = (bf16[64,8,512]{2,1,0:T(8,128)(2,1)}, bf16[64,8,512]{2,1,0:T(8,128)(2,1)}, f32[7,64,64]{2,1,0:T(8,128)}, f32[512,256]{1,0:T(8,128)}, f32[256,512]{1,...) custom-call(bf16[64,8,512]{2,1,0:T(8,128)(2,1)} %get-tuple-element.29.fine_in, ...), custom_call_target="tpu_custom_call" | custom-call | tf_op jit(solution)/shard_map/finish/pallas_call | solution.py:852
